TPU v7x, 32 devices: a whole 2x2x4 slice. The times are simulated.
32 devices in a mesh: layer: 8 (over y, x, core), dp: 4 (over z).
Axes of the slice: x: 2, y: 2, z: 4, core: 2. Of those that a mesh axis runs over, the one named last changes fastest.
Arguments:
- states: bfloat16 [64, 8, 64, 256], P('layer', 'dp'), may hold values from -6 to 6
- kernels: bfloat16 [64, 9, 64, 64], P('layer'), may hold values from -0.25 to 0.25
- boundary: float32 [8, 8, 64, 256], P('layer', 'dp'), may hold values from -6 to 6
Outputs:
- corrected: float32 [8, 8, 64, 256], P('layer', 'dp')
- bottoms: float32 [8, 8, 64, 256], P('layer', 'dp')
- gradients: float32 [64, 9, 64, 64], P('layer')
All inputs are finite; a program needn't handle non-finite values.
Results may differ from a plain program's by a relative error of at most 0.012.
Values may be sent and summed in bfloat16 or wider, within the bound.
A program may use at most 64 MiB of HBM per device.

v0:
```python
import functools

import jax
import jax.numpy as jnp
from jax import lax
from jax.experimental import pallas as pl
from jax.experimental.pallas import tpu as pltpu
from jax.sharding import PartitionSpec as P

MAP = 16
CELLS = MAP * MAP
LD = 8
CH = 64
STEP = 0.5 / LD
MESH_ID = pl.DeviceIdType.MESH
f32, bf16 = jnp.float32, jnp.bfloat16


def kernel(blocks, parts, samples, states, kernels, boundary, corrected, bottoms, grads,
           weights, slopes, acts, act_rows, mean_own, means, src_own, srcs,
           adj, chain, swap_out, swap_in, own, from_outer, half, from_across, whole, from_inner,
           mean_send, mean_recv, fwd_send, src_send, src_recv, swap_send, swap_recv,
           a_send, a_recv, b_send, b_recv, c_send, c_recv):
    me = lax.axis_index("layer")
    dp = lax.axis_index("dp")
    lanes = samples * CELLS
    width = lanes // 2
    core = lax.rem(me, 2)
    base = me - core
    other = me + 1 - 2 * core
    last = base == blocks - 2

    barrier = pltpu.get_barrier_semaphore()
    for i in range(1, blocks):
        pl.semaphore_signal(barrier, inc=1, device_id=(lax.rem(me + i, blocks), dp), device_id_type=MESH_ID)
    for i in range(1, parts):
        pl.semaphore_signal(barrier, inc=1, device_id=(me, lax.rem(dp + i, parts)), device_id_type=MESH_ID)

    cell = lax.broadcasted_iota(jnp.int32, (CH, lanes), 1)
    col = lax.bitwise_and(cell, MAP - 1)
    row = lax.bitwise_and(lax.shift_right_logical(cell, 4), MAP - 1)
    col_lo, col_hi = col >= 1, col <= MAP - 2
    row_lo, row_hi = row >= 1, row <= MAP - 2

    def cols(v):
        size = v.shape[1]
        left = jnp.where(col_hi[:, :size], pltpu.roll(v, size - 1, 1), 0.0)
        right = jnp.where(col_lo[:, :size], pltpu.roll(v, 1, 1), 0.0)
        return jnp.concatenate([left.astype(bf16), v.astype(bf16), right.astype(bf16)], axis=0)

    def rows_up(v):
        return jnp.where(row_hi[:, :v.shape[1]], pltpu.roll(v, v.shape[1] - MAP, 1), 0.0)

    def rows_down(v):
        return jnp.where(row_lo[:, :v.shape[1]], pltpu.roll(v, MAP, 1), 0.0)

    def conv(w, v):
        r = jnp.dot(w, v, preferred_element_type=f32)
        return rows_up(r[:CH]) + r[CH:2 * CH] + rows_down(r[2 * CH:])

    def flat(ref):
        return jnp.concatenate([ref[n] for n in range(samples)], axis=1)

    def turned(ks):
        return jnp.concatenate([k.astype(f32) for k in ks], axis=1).T.astype(bf16)

    total = [kernels[0, a].astype(f32) for a in range(3)]
    for l in range(1, LD):
        for a in range(3):
            total[a] = total[a] + kernels[l, a].astype(f32)
    mean = turned([t * (1.0 / LD) for t in total])
    mean_own[:3 * CH] = mean[:, :2 * CH]
    mean_own[3 * CH:] = jnp.concatenate([mean[:3 * CH // 2, 2 * CH:], mean[3 * CH // 2:, 2 * CH:]], axis=1)

    def unpacked(m):
        tail = jnp.concatenate([m[3 * CH:, :CH], m[3 * CH:, CH:]], axis=0)
        return jnp.concatenate([m[:3 * CH], tail], axis=1)

    pl.semaphore_wait(barrier, blocks - 1 + parts - 1)

    def mean_copy(peer):
        return pltpu.make_async_remote_copy(
            src_ref=mean_own, dst_ref=means.at[me], send_sem=mean_send.at[peer],
            recv_sem=mean_recv.at[me], device_id=(peer, dp), device_id_type=MESH_ID)

    def src_copy(peer, part):
        return pltpu.make_async_remote_copy(
            src_ref=src_own.at[part], dst_ref=srcs.at[me], send_sem=src_send.at[peer],
            recv_sem=src_recv.at[me], device_id=(peer, dp), device_id_type=MESH_ID)

    def mean_arrival(j):
        return pltpu.make_async_remote_copy(
            src_ref=mean_own, dst_ref=means.at[j], send_sem=mean_send.at[0],
            recv_sem=mean_recv.at[j], device_id=(other, dp), device_id_type=MESH_ID)

    def src_arrival(j):
        return pltpu.make_async_remote_copy(
            src_ref=src_own.at[0], dst_ref=srcs.at[j], send_sem=src_send.at[0],
            recv_sem=src_recv.at[j], device_id=(other, dp), device_id_type=MESH_ID)

    swap = pltpu.make_async_remote_copy(
        src_ref=swap_out, dst_ref=swap_in, send_sem=swap_send, recv_sem=swap_recv,
        device_id=(other, dp), device_id_type=MESH_ID)

    def forward(j):
        return pltpu.make_async_remote_copy(
            src_ref=means.at[j], dst_ref=means.at[j], send_sem=fwd_send.at[j],
            recv_sem=mean_recv.at[j], device_id=(other, dp), device_id_type=MESH_ID)

    for lower in range(0, blocks - 2, 2):
        @pl.when(jnp.logical_and(base > lower, me < blocks - 1))
        def _():
            mean_copy(lower + core).start()

    @pl.when(jnp.logical_and(core == 1, me < blocks - 1))
    def _():
        mean_copy(me - 1).start()

    top = flat(boundary.at[0])
    p = top
    for l in reversed(range(LD)):
        weights[l] = turned([kernels[l, a] for a in range(3)])
        h = jnp.tanh(flat(states.at[l]).astype(f32))
        slope = STEP * (1.0 - h * h)
        acts[l] = h.astype(bf16)
        slopes[l] = slope
        p = p + slope * conv(weights[l], cols(p))
    coarse = top + 0.5 * conv(mean, cols(top))
    source = p - jnp.where(me == blocks - 1, 0.0, coarse)
    for part in range(2):
        src_own[part] = source[:, part * width:(part + 1) * width].astype(bf16)

    @pl.when(core == 1)
    def _():
        src_copy(me - 1, 0).start()

    for peer in range(blocks - 2):
        @pl.when(base > peer)
        def _():
            src_copy(peer, peer % 2).start()

    @pl.when(jnp.logical_and(last, core == 1))
    def _():
        swap_out[...] = source[:, width:]
        swap.start()

    for j in reversed(range(2, blocks - 1)):
        @pl.when(jnp.logical_and(base + 1 < j, core == j % 2))
        def _():
            mean_arrival(j).wait_recv()
            forward(j).start()

    for l in range(LD):
        h = acts[l].astype(f32)
        act_rows[l] = jnp.concatenate(
            [rows_down(h).astype(bf16), h.astype(bf16), rows_up(h).astype(bf16)], axis=0)

    @pl.when(last)
    def _():
        @pl.when(core == 1)
        def _():
            adj[...] = top

        @pl.when(core == 0)
        def _():
            src_arrival(blocks - 1).wait_recv()
            adj[:, :width] = srcs[blocks - 1].astype(f32)
            swap.wait_recv()
            adj[:, width:] = swap_in[...]

    @pl.when(jnp.logical_not(last))
    def _():
        src_arrival(blocks - 1).wait_recv()
        chain[...] = srcs[blocks - 1].astype(f32)

    for j in reversed(range(2, blocks - 1)):
        @pl.when(jnp.logical_and(base + 1 < j, core != j % 2))
        def _():
            mean_arrival(j).wait_recv()

        @pl.when(base + 1 < j)
        def _():
            e = chain[...]
            e = e + 0.5 * conv(unpacked(means[j]), cols(e))
            src_arrival(j).wait_recv()
            chain[...] = e + srcs[j].astype(f32)

    @pl.when(jnp.logical_and(jnp.logical_not(last), core == 0))
    def _():
        e = chain[...]
        swap_out[...] = e
        swap.start()
        mean_arrival(me + 1).wait_recv()
        src_arrival(me + 1).wait_recv()
        adj[:, :width] = e + 0.5 * conv(unpacked(means[me + 1]), cols(e)) + srcs[me + 1].astype(f32)
        swap.wait_recv()
        adj[:, width:] = swap_in[...]

    @pl.when(jnp.logical_and(jnp.logical_not(last), core == 1))
    def _():
        e = chain[...]
        swap_out[...] = e + 0.5 * conv(unpacked(mean_own[...]), cols(e)) + src_own[1].astype(f32)
        swap.start()
        adj[:, width:] = e
        swap.wait_recv()
        adj[:, :width] = swap_in[...]

    p = adj[...]
    for n in range(samples):
        corrected[0, n] = p[:, n * CELLS:(n + 1) * CELLS]

    scale = STEP / (samples * parts)
    chunks = 3 * LD // 2
    inner = jnp.logical_or(dp == 1, dp == 2)
    outer = jnp.logical_or(dp == 0, dp == 3)
    mate = dp + 1 - 2 * lax.rem(dp, 2)
    across = 3 - dp

    def hop(src, dst, send, recv, c, peer):
        return pltpu.make_async_remote_copy(
            src_ref=src.at[c], dst_ref=dst.at[c], send_sem=send.at[c], recv_sem=recv.at[c],
            device_id=(me, peer), device_id_type=MESH_ID)

    def to_inner(c):
        return hop(own, from_outer, a_send, a_recv, c, mate)

    def to_across(c):
        return hop(half, from_across, b_send, b_recv, c, across)

    def to_outer(c):
        return hop(whole, from_inner, c_send, c_recv, c, mate)

    def put(c, v):
        g, k = c // 3, c % 3
        l = LD - 1 - 2 * g
        v = v.astype(f32)
        if k < 2:
            grads[l - k, 0] = v[:, :CH]
            grads[l - k, 1] = v[:, CH:]
        else:
            grads[l, 2] = v[:, :CH]
            grads[l - 1, 2] = v[:, CH:]

    def pair_sum(c):
        to_inner(c).wait_recv()
        half[c] = (own[c].astype(f32) + from_outer[c].astype(f32)).astype(bf16)
        to_across(c).start()

    def full_sum(c):
        to_across(c).wait_recv()
        v = (half[c].astype(f32) + from_across[c].astype(f32)).astype(bf16)
        whole[c] = v
        to_outer(c).start()
        put(c, v)

    paired, summed = 0, 0
    for i in range(LD):
        l = LD - 1 - i
        v = cols(p)
        p = p + slopes[l] * conv(weights[l], v)
        t = lax.dot_general(v, act_rows[l], (((1,), (1,)), ((), ())), preferred_element_type=f32) * scale
        c = 3 * (i // 2) + i % 2
        own[c] = t[:, :2 * CH].astype(bf16)
        ready = [c]
        if i % 2 == 0:
            kept = t[:, 2 * CH:]
        else:
            own[c + 1] = jnp.concatenate([kept, t[:, 2 * CH:]], axis=1).astype(bf16)
            ready.append(c + 1)

        @pl.when(outer)
        def _():
            for r in ready:
                to_inner(r).start()

        if i >= 2:
            @pl.when(inner)
            def _():
                pair_sum(i - 2)
                if i >= 4:
                    full_sum(i - 4)
    for n in range(samples):
        bottoms[0, n] = p[:, n * CELLS:(n + 1) * CELLS]

    @pl.when(inner)
    def _():
        for c in range(LD - 2, chunks):
            pair_sum(c)
            full_sum(c - 2)
        for c in range(chunks - 2, chunks):
            full_sum(c)
        for c in range(chunks):
            to_across(c).wait_send()
            to_outer(c).wait_send()

    @pl.when(outer)
    def _():
        for c in range(chunks):
            to_outer(c).wait_recv()
            put(c, from_inner[c])
        for c in range(chunks):
            to_inner(c).wait_send()

    for lower in range(0, blocks - 2, 2):
        @pl.when(jnp.logical_and(base > lower, me < blocks - 1))
        def _():
            mean_copy(lower + core).wait_send()

    @pl.when(jnp.logical_and(core == 1, me < blocks - 1))
    def _():
        mean_copy(me - 1).wait_send()

    for j in range(2, blocks - 1):
        @pl.when(jnp.logical_and(base + 1 < j, core == j % 2))
        def _():
            forward(j).wait_send()

    for peer in range(blocks - 2):
        @pl.when(base > peer)
        def _():
            src_copy(peer, peer % 2).wait_send()

    @pl.when(core == 1)
    def _():
        src_copy(me - 1, 0).wait_send()

    @pl.when(jnp.logical_or(jnp.logical_not(last), core == 1))
    def _():
        swap.wait_send()


def body(blocks, parts, states, kernels, boundary):
    samples = states.shape[1]
    lanes = samples * CELLS
    chunks = 3 * LD // 2
    vmem = pl.BlockSpec(memory_space=pltpu.VMEM)
    dma = pltpu.SemaphoreType.DMA
    corrected, bottoms, grads = pl.pallas_call(
        functools.partial(kernel, blocks, parts, samples),
        out_shape=(
            jax.ShapeDtypeStruct(boundary.shape, f32),
            jax.ShapeDtypeStruct(boundary.shape, f32),
            jax.ShapeDtypeStruct((LD, 3, 3 * CH, CH), f32),
        ),
        in_specs=[vmem] * 3,
        out_specs=(vmem,) * 3,
        scratch_shapes=[
            pltpu.VMEM((LD, 3 * CH, 3 * CH), bf16),
            pltpu.VMEM((LD, CH, lanes), f32),
            pltpu.VMEM((LD, CH, lanes), bf16),
            pltpu.VMEM((LD, 3 * CH, lanes), bf16),
            pltpu.VMEM((9 * CH // 2, 2 * CH), bf16),
            pltpu.VMEM((blocks, 9 * CH // 2, 2 * CH), bf16),
            pltpu.VMEM((2, CH, lanes // 2), bf16),
            pltpu.VMEM((blocks, CH, lanes // 2), bf16),
            pltpu.VMEM((CH, lanes), f32),
            *[pltpu.VMEM((CH, lanes // 2), f32)] * 3,
            *[pltpu.VMEM((chunks, 3 * CH, 2 * CH), bf16)] * 6,
            *[dma((blocks,))] * 5, dma, dma,
            *[dma((chunks,))] * 6,
        ],
        compiler_params=pltpu.CompilerParams(
            collective_id=0, has_side_effects=True, vmem_limit_bytes=40 * 1024 * 1024),
        cost_estimate=pl.CostEstimate(flops=2 * 10**9, bytes_accessed=6 * 10**6, transcendentals=262144),
        name="cycle",
    )(states, kernels.reshape(LD, 3, 3 * CH, CH), boundary)
    return corrected, bottoms, grads.reshape(LD, 9, CH, CH)


def solution(mesh):
    placed = (
        P("layer", "dp", None, None),
        P("layer", None, None, None),
        P("layer", "dp", None, None),
    )
    return jax.shard_map(
        functools.partial(body, mesh.shape["layer"], mesh.shape["dp"]),
        mesh=mesh,
        in_specs=placed,
        out_specs=(
            P("layer", "dp", None, None),
            P("layer", "dp", None, None),
            P("layer", None, None, None),
        ),
        check_vma=False,
    )
```

profile of v0, /device:TPU:0, one launch (start us, length us, event | category | flops | bytes accessed | tf_op | source)
XLA Modules:
  0.0 46.7 jit_solution(17006750073190560491)
XLA Ops:
  0.6 0.0 copy-start
  0.6 1.3 %copy-done = bf16[8,9,64,64]{3,2,1,0:T(8,128)(2,1)S(1)} copy-done((bf16[8,9,64,64]{3,2,1,0:T(8,128)(2,1)S(1)}, bf16[8,9,64,64]{3,2,1,0:T(8,128)(2,1)}, u32[]{:S(2)}) %copy-start) | copy-done | bytes 589848
  1.9 0.0 copy-start.1
  1.9 1.0 %copy-done.1 = bf16[8,2,64,256]{3,2,1,0:T(8,128)(2,1)S(1)} copy-done((bf16[8,2,64,256]{3,2,1,0:T(8,128)(2,1)S(1)}, bf16[8,2,64,256]{3,2,1,0:T(8,128)(2,1)}, u32[]{:S(2)}) %copy-start.1) | copy-done | bytes 524312
  2.9 0.0 copy-start.2
  2.9 0.9 %copy-done.2 = f32[1,2,64,256]{3,2,1,0:T(8,128)S(1)} copy-done((f32[1,2,64,256]{3,2,1,0:T(8,128)S(1)}, f32[1,2,64,256]{3,2,1,0:T(8,128)}, u32[]{:S(2)}) %copy-start.2) | copy-done | bytes 131096
  3.8 40.1 %cycle.1 = (f32[1,2,64,256]{3,2,1,0:T(8,128)S(1)}, f32[1,2,64,256]{3,2,1,0:T(8,128)S(1)}, f32[8,3,192,64]{3,2,1,0:T(8,128)S(1)}) custom-call(bf16[8,2,64,256]{3,2,1,0:T(8,128)(2,1)S(1)} %copy-done.1, bf16[8,3,192,64]{3,2,1,0:T(8,128)(2,1)S(1)} %bitcast.3, f32[1,2,64,256]{3,2,1,0:T(8,128)S(1)} %copy-done.2), custom_call_target="tpu_custom_call" | custom-call | flops 2000000000 | bytes 6000000 | tf_op jit(solution)/shard_map/cycle/pallas_call | solution.py:338
  44.0 0.7 %copy.9 = f32[1,2,64,256]{3,2,1,0:T(8,128)} copy(f32[1,2,64,256]{3,2,1,0:T(8,128)S(1)} %get-tuple-element.12) | data formatting | bytes 262144
  44.7 0.7 %copy.10 = f32[1,2,64,256]{3,2,1,0:T(8,128)} copy(f32[1,2,64,256]{3,2,1,0:T(8,128)S(1)} %get-tuple-element.13) | data formatting | bytes 262144
  45.3 1.4 %copy.11 = f32[8,9,64,64]{3,2,1,0:T(8,128)} copy(f32[8,9,64,64]{3,2,1,0:T(8,128)S(1)} %bitcast.2) | data formatting | bytes 2359296
Async XLA Ops:
  0.6 1.3 %copy-start = (bf16[8,9,64,64]{3,2,1,0:T(8,128)(2,1)S(1)}, bf16[8,9,64,64]{3,2,1,0:T(8,128)(2,1)}, u32[]{:S(2)}) copy-start(bf16[8,9,64,64]{3,2,1,0:T(8,128)(2,1)} %param.4) | copy-start | bytes 1769476
  1.9 1.0 %copy-start.1 = (bf16[8,2,64,256]{3,2,1,0:T(8,128)(2,1)S(1)}, bf16[8,2,64,256]{3,2,1,0:T(8,128)(2,1)}, u32[]{:S(2)}) copy-start(bf16[8,2,64,256]{3,2,1,0:T(8,128)(2,1)} %states.1) | copy-start | bytes 1572868
  2.9 0.9 %copy-start.2 = (f32[1,2,64,256]{3,2,1,0:T(8,128)S(1)}, f32[1,2,64,256]{3,2,1,0:T(8,128)}, u32[]{:S(2)}) copy-start(f32[1,2,64,256]{3,2,1,0:T(8,128)} %boundary.1) | copy-start | bytes 393220
where the time goes:
time: 46.9 us; the launch traced here: 46.7 us
  Pallas kernels  40.1 us (86%)
  local copies, waits for them, and re-layouts  5.93 us (13%)
  between operations  0.65 us (1%)
    pallas_call x1, Pallas kernels, body(): pl.pallas_call(functools.partial(kernel, blocks, parts, samples), out_sha...  40.1 us
    unnamed x9, local copies, waits for them, and re-layouts  5.93 us

commit v1 on v0

--- a/solution.py
+++ b/solution.py
@@ -16,8 +16,8 @@
 f32, bf16 = jnp.float32, jnp.bfloat16
 
 
-def kernel(blocks, parts, samples, states, kernels, boundary, corrected, bottoms, grads,
-           weights, slopes, acts, act_rows, mean_own, means, src_own, srcs,
+def kernel(blocks, parts, samples, states_in, kernels_in, boundary_in, corrected, bottoms, grads,
+           states, kernels, boundary, in_sem, weights, slopes, acts, act_rows, mean_own, means, src_own, srcs,
            adj, chain, swap_out, swap_in, own, from_outer, half, from_across, whole, from_inner,
            mean_send, mean_recv, fwd_send, src_send, src_recv, swap_send, swap_recv,
            a_send, a_recv, b_send, b_recv, c_send, c_recv):
@@ -36,6 +36,12 @@
     for i in range(1, parts):
         pl.semaphore_signal(barrier, inc=1, device_id=(me, lax.rem(dp + i, parts)), device_id_type=MESH_ID)
 
+    loads = [pltpu.make_async_copy(kernels_in, kernels, in_sem.at[0]),
+             pltpu.make_async_copy(boundary_in, boundary, in_sem.at[1]),
+             pltpu.make_async_copy(states_in, states, in_sem.at[2])]
+    for load in loads:
+        load.start()
+
     cell = lax.broadcasted_iota(jnp.int32, (CH, lanes), 1)
     col = lax.bitwise_and(cell, MAP - 1)
     row = lax.bitwise_and(lax.shift_right_logical(cell, 4), MAP - 1)
@@ -64,6 +70,7 @@
     def turned(ks):
         return jnp.concatenate([k.astype(f32) for k in ks], axis=1).T.astype(bf16)
 
+    loads[0].wait()
     total = [kernels[0, a].astype(f32) for a in range(3)]
     for l in range(1, LD):
         for a in range(3):
@@ -116,6 +123,8 @@
     def _():
         mean_copy(me - 1).start()
 
+    loads[1].wait()
+    loads[2].wait()
     top = flat(boundary.at[0])
     p = top
     for l in reversed(range(LD)):
@@ -329,11 +338,22 @@
         swap.wait_send()
 
 
+def write(corrected, bottoms, grads, corrected_out, bottoms_out, grads_out, sem):
+    stores = [pltpu.make_async_copy(grads, grads_out, sem.at[0]),
+              pltpu.make_async_copy(corrected, corrected_out, sem.at[1]),
+              pltpu.make_async_copy(bottoms, bottoms_out, sem.at[2])]
+    for store in stores:
+        store.start()
+    for store in stores:
+        store.wait()
+
+
 def body(blocks, parts, states, kernels, boundary):
     samples = states.shape[1]
     lanes = samples * CELLS
     chunks = 3 * LD // 2
     vmem = pl.BlockSpec(memory_space=pltpu.VMEM)
+    hbm = pl.BlockSpec(memory_space=pltpu.HBM)
     dma = pltpu.SemaphoreType.DMA
     corrected, bottoms, grads = pl.pallas_call(
         functools.partial(kernel, blocks, parts, samples),
@@ -342,9 +362,13 @@
             jax.ShapeDtypeStruct(boundary.shape, f32),
             jax.ShapeDtypeStruct((LD, 3, 3 * CH, CH), f32),
         ),
-        in_specs=[vmem] * 3,
+        in_specs=[hbm] * 3,
         out_specs=(vmem,) * 3,
         scratch_shapes=[
+            pltpu.VMEM(states.shape, bf16),
+            pltpu.VMEM((LD, 3, 3 * CH, CH), bf16),
+            pltpu.VMEM(boundary.shape, f32),
+            dma((3,)),
             pltpu.VMEM((LD, 3 * CH, 3 * CH), bf16),
             pltpu.VMEM((LD, CH, lanes), f32),
             pltpu.VMEM((LD, CH, lanes), bf16),
@@ -363,7 +387,18 @@
             collective_id=0, has_side_effects=True, vmem_limit_bytes=40 * 1024 * 1024),
         cost_estimate=pl.CostEstimate(flops=2 * 10**9, bytes_accessed=6 * 10**6, transcendentals=262144),
         name="cycle",
-    )(states, kernels.reshape(LD, 3, 3 * CH, CH), boundary)
+    )(*[pltpu.with_memory_space_constraint(a, pltpu.HBM) for a in (states, kernels.reshape(LD, 3, 3 * CH, CH), boundary)])
+    shapes = (corrected, bottoms, grads)
+    corrected, bottoms, grads = pl.pallas_call(
+        write,
+        out_shape=tuple(jax.ShapeDtypeStruct(a.shape, a.dtype) for a in shapes),
+        in_specs=[pl.BlockSpec(memory_space=pl.ANY)] * 3,
+        out_specs=(hbm,) * 3,
+        scratch_shapes=[dma((3,))],
+        cost_estimate=pl.CostEstimate(flops=0, bytes_accessed=5 * 10**6, transcendentals=0),
+        compiler_params=pltpu.CompilerParams(vmem_limit_bytes=4 * 1024 * 1024),
+        name="write",
+    )(*[pltpu.with_memory_space_constraint(a, pltpu.VMEM) for a in shapes])
     return corrected, bottoms, grads.reshape(LD, 9, CH, CH)
 
 

time: 46.9 us -> 42.4 us (0.904)
  local copies, waits for them, and re-layouts: 5.93 us -> 0 us
  Pallas kernels: 40.1 us -> 41.7 us
    unnamed x9 -> x0, local copies, waits for them, and re-layouts: 5.93 us -> none
    pallas_call x0 -> x1, Pallas kernels: none -> 1.5 us  [body(): pl.pallas_call(write, out_shape=tuple((jax.ShapeDtypeStruct(a.shape, a.dt...]
where the time goes in v1:
time: 42.4 us; the launch traced here: 42.3 us
  Pallas kernels  41.7 us (98%)
  between operations  0.64 us (2%)
    pallas_call x1, Pallas kernels, body(): pl.pallas_call(functools.partial(kernel, blocks, parts, samples), out_sha...  40.2 us
    pallas_call x1, Pallas kernels, body(): pl.pallas_call(write, out_shape=tuple((jax.ShapeDtypeStruct(a.shape, a.dt...  1.5 us

profile of v1, /device:TPU:0, one launch (start us, length us, event | category | flops | bytes accessed | tf_op | source)
XLA Modules:
  0.0 42.3 jit_solution(450229063120458890)
XLA Ops:
  0.6 40.2 %cycle.1 = (f32[1,2,64,256]{3,2,1,0:T(8,128)S(1)}, f32[1,2,64,256]{3,2,1,0:T(8,128)S(1)}, f32[8,3,192,64]{3,2,1,0:T(8,128)S(1)}) custom-call(bf16[8,2,64,256]{3,2,1,0:T(8,128)(2,1)} %states_in.1, bf16[8,3,192,64]{3,2,1,0:T(8,128)(2,1)} %bitcast.3, f32[1,2,64,256]{3,2,1,0:T(8,128)} %boundary_in.1), custom_call_target="tpu_custom_call" | custom-call | flops 2000000000 | bytes 6000000 | tf_op jit(solution)/shard_map/cycle/pallas_call | solution.py:358
  40.8 1.5 %write.1 = (f32[1,2,64,256]{3,2,1,0:T(8,128)}, f32[1,2,64,256]{3,2,1,0:T(8,128)}, f32[8,3,192,64]{3,2,1,0:T(8,128)}) custom-call(f32[1,2,64,256]{3,2,1,0:T(8,128)S(1)} %get-tuple-element.9.corrected, f32[1,2,64,256]{3,2,1,0:T(8,128)S(1)} %get-tuple-element.10.bottoms, f32[8,3,192,64]{3,2,1,0:T(8,128)S(1)} %get-tuple-element.11.grads), custom_call_target="tpu_custom_call" | custom-call | bytes 5000000 | tf_op jit(solution)/shard_map/write/pallas_call | solution.py:392

commit v2 on v1

--- a/solution.py
+++ b/solution.py
@@ -12,14 +12,18 @@
 LD = 8
 CH = 64
 STEP = 0.5 / LD
+M = 3
+PIECES = 1
+PACKED = 9 * CH // 2
+PIECE = PACKED // PIECES
 MESH_ID = pl.DeviceIdType.MESH
 f32, bf16 = jnp.float32, jnp.bfloat16
 
 
 def kernel(blocks, parts, samples, states_in, kernels_in, boundary_in, corrected, bottoms, grads,
            states, kernels, boundary, in_sem, weights, slopes, acts, act_rows, mean_own, means, src_own, srcs,
-           adj, chain, swap_out, swap_in, own, from_outer, half, from_across, whole, from_inner,
-           mean_send, mean_recv, fwd_send, src_send, src_recv, swap_send, swap_recv,
+           adj, chain, swap_out, swap_in, far, adjs, rep, own, from_outer, half, from_across, whole, from_inner,
+           far_send, far_recv, adj_send, adj_recv, mean_send, mean_recv, fwd_send, src_send, src_recv, swap_send, swap_recv,
            a_send, a_recv, b_send, b_recv, c_send, c_recv):
     me = lax.axis_index("layer")
     dp = lax.axis_index("dp")
@@ -29,6 +33,11 @@
     base = me - core
     other = me + 1 - 2 * core
     last = base == blocks - 2
+    inner = jnp.logical_or(dp == 1, dp == 2)
+    outer = jnp.logical_or(dp == 0, dp == 3)
+    mate = dp + 1 - 2 * lax.rem(dp, 2)
+    across = 3 - dp
+    near = lax.div(dp, 2)
 
     barrier = pltpu.get_barrier_semaphore()
     for i in range(1, blocks):
@@ -42,7 +51,7 @@
     for load in loads:
         load.start()
 
-    cell = lax.broadcasted_iota(jnp.int32, (CH, lanes), 1)
+    cell = lax.broadcasted_iota(jnp.int32, (CH, 2 * lanes), 1)
     col = lax.bitwise_and(cell, MAP - 1)
     row = lax.bitwise_and(lax.shift_right_logical(cell, 4), MAP - 1)
     col_lo, col_hi = col >= 1, col <= MAP - 2
@@ -105,6 +114,46 @@
             src_ref=src_own.at[0], dst_ref=srcs.at[j], send_sem=src_send.at[0],
             recv_sem=src_recv.at[j], device_id=(other, dp), device_id_type=MESH_ID)
 
+    def far_copy(src, s, i, n, peer):
+        return pltpu.make_async_remote_copy(
+            src_ref=src, dst_ref=far.at[s, i], send_sem=far_send.at[n, i], recv_sem=far_recv.at[s, i],
+            device_id=(me, peer), device_id_type=MESH_ID)
+
+    def far_sends(i):
+        src = states.at[LD - 1 - i]
+        return far_copy(src, dp, i, 0, 2 - near), far_copy(src, dp, i, 1, mate)
+
+    def far_forward(i, n):
+        s = across if n == 2 else 3 - mate
+        return far_copy(far.at[s, i], s, i, n, mate)
+
+    def far_arrival(s, i):
+        return far_copy(far.at[s, i], s, i, 0, mate)
+
+    def adj_copy(s, n, peer):
+        return pltpu.make_async_remote_copy(
+            src_ref=adjs.at[s], dst_ref=adjs.at[s], send_sem=adj_send.at[n], recv_sem=adj_recv.at[s],
+            device_id=(me, peer), device_id_type=MESH_ID)
+
+    def adj_to_mate():
+        return adj_copy(dp, 0, mate)
+
+    def adj_to_across():
+        return adj_copy(dp, 1, across)
+
+    def adj_forwards():
+        return adj_copy(mate, 2, across), adj_copy(across, 3, mate), adj_copy(3 - mate, 4, mate)
+
+    forwards = [(i, n) for i in range(M) for n in (2, 3)]
+
+    def pass_on(count):
+        for i, n in forwards[:count]:
+            @pl.when(inner)
+            def _():
+                far_arrival(across if n == 2 else 3 - mate, i).wait_recv()
+                far_forward(i, n).start()
+        del forwards[:count]
+
     swap = pltpu.make_async_remote_copy(
         src_ref=swap_out, dst_ref=swap_in, send_sem=swap_send, recv_sem=swap_recv,
         device_id=(other, dp), device_id_type=MESH_ID)
@@ -123,8 +172,13 @@
     def _():
         mean_copy(me - 1).start()
 
+    loads[2].wait()
+    for i in range(M):
+        for copy in far_sends(i):
+            copy.start()
+        far[dp, i] = states[LD - 1 - i]
+
     loads[1].wait()
-    loads[2].wait()
     top = flat(boundary.at[0])
     p = top
     for l in reversed(range(LD)):
@@ -159,7 +213,8 @@
             mean_arrival(j).wait_recv()
             forward(j).start()
 
-    for l in range(LD):
+    pass_on(1)
+    for l in range(LD - M):
         h = acts[l].astype(f32)
         act_rows[l] = jnp.concatenate(
             [rows_down(h).astype(bf16), h.astype(bf16), rows_up(h).astype(bf16)], axis=0)
@@ -183,6 +238,8 @@
         chain[...] = srcs[blocks - 1].astype(f32)
 
     for j in reversed(range(2, blocks - 1)):
+        pass_on(1)
+
         @pl.when(jnp.logical_and(base + 1 < j, core != j % 2))
         def _():
             mean_arrival(j).wait_recv()
@@ -215,19 +272,23 @@
         adj[:, :width] = swap_in[...]
 
     p = adj[...]
+    adjs[dp] = p.astype(bf16)
+    adj_to_mate().start()
+
+    @pl.when(inner)
+    def _():
+        adj_to_across().start()
+
     for n in range(samples):
         corrected[0, n] = p[:, n * CELLS:(n + 1) * CELLS]
 
     scale = STEP / (samples * parts)
-    chunks = 3 * LD // 2
-    inner = jnp.logical_or(dp == 1, dp == 2)
-    outer = jnp.logical_or(dp == 0, dp == 3)
-    mate = dp + 1 - 2 * lax.rem(dp, 2)
-    across = 3 - dp
+    chunks = (LD - M) * PIECES
 
     def hop(src, dst, send, recv, c, peer):
-        return pltpu.make_async_remote_copy(
-            src_ref=src.at[c], dst_ref=dst.at[c], send_sem=send.at[c], recv_sem=recv.at[c],
+        part = (c // PIECES, pl.ds(c % PIECES * PIECE, PIECE))
+        return pltpu.make_async_remote_copy(
+            src_ref=src.at[part], dst_ref=dst.at[part], send_sem=send.at[c], recv_sem=recv.at[c],
             device_id=(me, peer), device_id_type=MESH_ID)
 
     def to_inner(c):
@@ -240,75 +301,133 @@
         return hop(whole, from_inner, c_send, c_recv, c, mate)
 
     def put(c, v):
-        g, k = c // 3, c % 3
-        l = LD - 1 - 2 * g
+        l = LD - M - 1 - c // PIECES
         v = v.astype(f32)
-        if k < 2:
-            grads[l - k, 0] = v[:, :CH]
-            grads[l - k, 1] = v[:, CH:]
-        else:
-            grads[l, 2] = v[:, :CH]
-            grads[l - 1, 2] = v[:, CH:]
+        start = c % PIECES * PIECE
+        full = min(max(3 * CH - start, 0), PIECE)
+        if full:
+            grads[l, 0, start:start + full] = v[:full, :CH]
+            grads[l, 1, start:start + full] = v[:full, CH:]
+        if full < PIECE:
+            low = start + full - 3 * CH
+            grads[l, 2, low:low + PIECE - full] = v[full:, :CH]
+            low = low + 3 * CH // 2
+            grads[l, 2, low:low + PIECE - full] = v[full:, CH:]
 
     def pair_sum(c):
+        part = (c // PIECES, pl.ds(c % PIECES * PIECE, PIECE))
         to_inner(c).wait_recv()
-        half[c] = (own[c].astype(f32) + from_outer[c].astype(f32)).astype(bf16)
+        half[part] = (own[part].astype(f32) + from_outer[part].astype(f32)).astype(bf16)
         to_across(c).start()
 
     def full_sum(c):
+        part = (c // PIECES, pl.ds(c % PIECES * PIECE, PIECE))
         to_across(c).wait_recv()
-        v = (half[c].astype(f32) + from_across[c].astype(f32)).astype(bf16)
-        whole[c] = v
+        v = (half[part].astype(f32) + from_across[part].astype(f32)).astype(bf16)
+        whole[part] = v
         to_outer(c).start()
         put(c, v)
 
-    paired, summed = 0, 0
+    def replicated(q, i):
+        l = LD - 1 - i
+        pair = (2 * q, 2 * q + 1)
+        if i == 0:
+            e = jnp.concatenate([adjs[s] for s in pair], axis=1).astype(f32)
+        else:
+            e = rep[...]
+        h = jnp.tanh(jnp.concatenate([far[s, i, n] for s in pair for n in range(samples)], axis=1).astype(f32))
+        v = cols(e)
+        if i < M - 1:
+            rep[...] = e + STEP * (1.0 - h * h) * conv(weights[l], v)
+        h = h.astype(bf16).astype(f32)
+        h = jnp.concatenate([rows_down(h).astype(bf16), h.astype(bf16), rows_up(h).astype(bf16)], axis=0)
+        return lax.dot_general(v, h, (((1,), (1,)), ((), ())), preferred_element_type=f32) * scale
+
     for i in range(LD):
         l = LD - 1 - i
         v = cols(p)
         p = p + slopes[l] * conv(weights[l], v)
-        t = lax.dot_general(v, act_rows[l], (((1,), (1,)), ((), ())), preferred_element_type=f32) * scale
-        c = 3 * (i // 2) + i % 2
-        own[c] = t[:, :2 * CH].astype(bf16)
-        ready = [c]
-        if i % 2 == 0:
-            kept = t[:, 2 * CH:]
-        else:
-            own[c + 1] = jnp.concatenate([kept, t[:, 2 * CH:]], axis=1).astype(bf16)
-            ready.append(c + 1)
-
-        @pl.when(outer)
-        def _():
-            for r in ready:
-                to_inner(r).start()
-
-        if i >= 2:
-            @pl.when(inner)
+        if i >= M:
+            t = lax.dot_general(v, act_rows[l], (((1,), (1,)), ((), ())), preferred_element_type=f32) * scale
+            own[i - M, :3 * CH] = t[:, :2 * CH].astype(bf16)
+            own[i - M, 3 * CH:] = jnp.concatenate(
+                [t[:3 * CH // 2, 2 * CH:], t[3 * CH // 2:, 2 * CH:]], axis=1).astype(bf16)
+
+            @pl.when(outer)
             def _():
-                pair_sum(i - 2)
-                if i >= 4:
-                    full_sum(i - 4)
+                for c in range((i - M) * PIECES, (i - M + 1) * PIECES):
+                    to_inner(c).start()
     for n in range(samples):
         bottoms[0, n] = p[:, n * CELLS:(n + 1) * CELLS]
 
+    adj_copy(mate, 0, mate).wait_recv()
+
     @pl.when(inner)
     def _():
-        for c in range(LD - 2, chunks):
-            pair_sum(c)
-            full_sum(c - 2)
-        for c in range(chunks - 2, chunks):
-            full_sum(c)
+        adj_forwards()[0].start()
+        adj_copy(across, 0, mate).wait_recv()
+        adj_forwards()[1].start()
+
+    pass_on(len(forwards))
+    for i in range(M):
+        far_arrival(mate, i).wait_recv()
+
+    lag = 2
+    for u in range(2 * M):
+        @pl.when(inner)
+        def _():
+            if u < chunks:
+                pair_sum(u)
+            if lag <= u < chunks + lag:
+                full_sum(u - lag)
+            if u == 1:
+                adj_copy(3 - mate, 0, mate).wait_recv()
+                adj_forwards()[2].start()
+
+        if u == M:
+            @pl.when(outer)
+            def _():
+                for s in (2 - 2 * near, 3 - 2 * near):
+                    adj_copy(s, 0, mate).wait_recv()
+                    for i in range(M):
+                        far_arrival(s, i).wait_recv()
+
+        l = LD - 1 - u % M
+        t = replicated(near if u < M else 1 - near, u % M)
+        for a in range(3):
+            g = t[:, a * CH:(a + 1) * CH]
+            grads[l, a] = g if u < M else grads[l, a] + g
+
+    @pl.when(inner)
+    def _():
+        for u in range(2 * M, chunks + lag):
+            if u < chunks:
+                pair_sum(u)
+            if u >= lag:
+                full_sum(u - lag)
         for c in range(chunks):
             to_across(c).wait_send()
             to_outer(c).wait_send()
+        adj_to_across().wait_send()
+        for copy in adj_forwards():
+            copy.wait_send()
+        for n in (2, 3):
+            for i in range(M):
+                far_forward(i, n).wait_send()
 
     @pl.when(outer)
     def _():
         for c in range(chunks):
             to_outer(c).wait_recv()
-            put(c, from_inner[c])
+            part = (c // PIECES, pl.ds(c % PIECES * PIECE, PIECE))
+            put(c, from_inner[part])
         for c in range(chunks):
             to_inner(c).wait_send()
+
+    adj_to_mate().wait_send()
+    for i in range(M):
+        for copy in far_sends(i):
+            copy.wait_send()
 
     for lower in range(0, blocks - 2, 2):
         @pl.when(jnp.logical_and(base > lower, me < blocks - 1))
@@ -351,7 +470,7 @@
 def body(blocks, parts, states, kernels, boundary):
     samples = states.shape[1]
     lanes = samples * CELLS
-    chunks = 3 * LD // 2
+    chunks = (LD - M) * PIECES
     vmem = pl.BlockSpec(memory_space=pltpu.VMEM)
     hbm = pl.BlockSpec(memory_space=pltpu.HBM)
     dma = pltpu.SemaphoreType.DMA
@@ -372,14 +491,18 @@
             pltpu.VMEM((LD, 3 * CH, 3 * CH), bf16),
             pltpu.VMEM((LD, CH, lanes), f32),
             pltpu.VMEM((LD, CH, lanes), bf16),
-            pltpu.VMEM((LD, 3 * CH, lanes), bf16),
+            pltpu.VMEM((LD - M, 3 * CH, lanes), bf16),
             pltpu.VMEM((9 * CH // 2, 2 * CH), bf16),
             pltpu.VMEM((blocks, 9 * CH // 2, 2 * CH), bf16),
             pltpu.VMEM((2, CH, lanes // 2), bf16),
             pltpu.VMEM((blocks, CH, lanes // 2), bf16),
             pltpu.VMEM((CH, lanes), f32),
             *[pltpu.VMEM((CH, lanes // 2), f32)] * 3,
-            *[pltpu.VMEM((chunks, 3 * CH, 2 * CH), bf16)] * 6,
+            pltpu.VMEM((parts, M, samples, CH, CELLS), bf16),
+            pltpu.VMEM((parts, CH, lanes), bf16),
+            pltpu.VMEM((CH, 2 * lanes), f32),
+            *[pltpu.VMEM((LD - M, PACKED, 2 * CH), bf16)] * 6,
+            dma((4, M)), dma((parts, M)), dma((5,)), dma((parts,)),
             *[dma((blocks,))] * 5, dma, dma,
             *[dma((chunks,))] * 6,
         ],

time: 42.4 us -> 37.9 us (0.89)
  Pallas kernels: 41.7 us -> 37.1 us
    pallas_call x1, Pallas kernels: 40.2 us -> 35.6 us  [body(): pl.pallas_call(functools.partial(kernel, blocks, parts, samples), out_sha...]
where the time goes in v2:
time: 37.9 us; the launch traced here: 37.7 us
  Pallas kernels  37.1 us (98%)
  between operations  0.64 us (2%)
    pallas_call x1, Pallas kernels, body(): pl.pallas_call(functools.partial(kernel, blocks, parts, samples), out_sha...  35.6 us
    pallas_call x1, Pallas kernels, body(): pl.pallas_call(write, out_shape=tuple((jax.ShapeDtypeStruct(a.shape, a.dt...  1.5 us

profile of v2, /device:TPU:0, one launch (start us, length us, event | category | flops | bytes accessed | tf_op | source)
XLA Modules:
  0.0 37.7 jit_solution(13429301797291016894)
XLA Ops:
  0.6 35.6 %cycle.1 = (f32[1,2,64,256]{3,2,1,0:T(8,128)S(1)}, f32[1,2,64,256]{3,2,1,0:T(8,128)S(1)}, f32[8,3,192,64]{3,2,1,0:T(8,128)S(1)}) custom-call(bf16[8,2,64,256]{3,2,1,0:T(8,128)(2,1)} %states_in.1, bf16[8,3,192,64]{3,2,1,0:T(8,128)(2,1)} %bitcast.3, f32[1,2,64,256]{3,2,1,0:T(8,128)} %boundary_in.1), custom_call_target="tpu_custom_call" | custom-call | flops 2000000000 | bytes 6000000 | tf_op jit(solution)/shard_map/cycle/pallas_call | solution.py:477
  36.2 1.5 %write.1 = (f32[1,2,64,256]{3,2,1,0:T(8,128)}, f32[1,2,64,256]{3,2,1,0:T(8,128)}, f32[8,3,192,64]{3,2,1,0:T(8,128)}) custom-call(f32[1,2,64,256]{3,2,1,0:T(8,128)S(1)} %get-tuple-element.9.corrected, f32[1,2,64,256]{3,2,1,0:T(8,128)S(1)} %get-tuple-element.10.bottoms, f32[8,3,192,64]{3,2,1,0:T(8,128)S(1)} %get-tuple-element.11.grads), custom_call_target="tpu_custom_call" | custom-call | bytes 5000000 | tf_op jit(solution)/shard_map/write/pallas_call | solution.py:515

commit v3 on v2

--- a/solution.py
+++ b/solution.py
@@ -12,8 +12,12 @@
 LD = 8
 CH = 64
 STEP = 0.5 / LD
-M = 3
-PIECES = 1
+MO = 3
+MI = 3
+PIECES = 2
+LAG = 5
+FWD = 3
+EARLY = 1
 PACKED = 9 * CH // 2
 PIECE = PACKED // PIECES
 MESH_ID = pl.DeviceIdType.MESH
@@ -21,7 +25,7 @@
 
 
 def kernel(blocks, parts, samples, states_in, kernels_in, boundary_in, corrected, bottoms, grads,
-           states, kernels, boundary, in_sem, weights, slopes, acts, act_rows, mean_own, means, src_own, srcs,
+           states, kernels, boundary, in_sem, mean_w, weights, slopes, acts, act_rows, mean_own, means, src_own, srcs,
            adj, chain, swap_out, swap_in, far, adjs, rep, own, from_outer, half, from_across, whole, from_inner,
            far_send, far_recv, adj_send, adj_recv, mean_send, mean_recv, fwd_send, src_send, src_recv, swap_send, swap_recv,
            a_send, a_recv, b_send, b_recv, c_send, c_recv):
@@ -51,33 +55,41 @@
     for load in loads:
         load.start()
 
-    cell = lax.broadcasted_iota(jnp.int32, (CH, 2 * lanes), 1)
-    col = lax.bitwise_and(cell, MAP - 1)
-    row = lax.bitwise_and(lax.shift_right_logical(cell, 4), MAP - 1)
+    cell = lax.broadcasted_iota(jnp.int32, (CH, CELLS), 1)
+    col = lax.bitwise_and(cell[:, :2 * CH], MAP - 1)
+    row = lax.shift_right_logical(cell, 4)
     col_lo, col_hi = col >= 1, col <= MAP - 2
     row_lo, row_hi = row >= 1, row <= MAP - 2
 
     def cols(v):
-        size = v.shape[1]
-        left = jnp.where(col_hi[:, :size], pltpu.roll(v, size - 1, 1), 0.0)
-        right = jnp.where(col_lo[:, :size], pltpu.roll(v, 1, 1), 0.0)
-        return jnp.concatenate([left.astype(bf16), v.astype(bf16), right.astype(bf16)], axis=0)
+        pieces = [v[:, k:k + 2 * CH] for k in range(0, v.shape[1], 2 * CH)]
+        left = [jnp.where(col_hi, pltpu.roll(x, 2 * CH - 1, 1), 0.0).astype(bf16) for x in pieces]
+        right = [jnp.where(col_lo, pltpu.roll(x, 1, 1), 0.0).astype(bf16) for x in pieces]
+        return jnp.concatenate(
+            [jnp.concatenate(left, axis=1), v.astype(bf16), jnp.concatenate(right, axis=1)], axis=0)
+
+    def by_sample(f, v):
+        return jnp.concatenate([f(v[:, k:k + CELLS]) for k in range(0, v.shape[1], CELLS)], axis=1)
 
     def rows_up(v):
-        return jnp.where(row_hi[:, :v.shape[1]], pltpu.roll(v, v.shape[1] - MAP, 1), 0.0)
+        return by_sample(lambda x: jnp.where(row_hi, pltpu.roll(x, CELLS - MAP, 1), 0.0), v)
 
     def rows_down(v):
-        return jnp.where(row_lo[:, :v.shape[1]], pltpu.roll(v, MAP, 1), 0.0)
+        return by_sample(lambda x: jnp.where(row_lo, pltpu.roll(x, MAP, 1), 0.0), v)
 
     def conv(w, v):
         r = jnp.dot(w, v, preferred_element_type=f32)
         return rows_up(r[:CH]) + r[CH:2 * CH] + rows_down(r[2 * CH:])
 
+    def step(ps, vs, l):
+        return [q + slopes[l, :, n * CELLS:(n + 1) * CELLS] * conv(weights[l], v)
+                for n, (q, v) in enumerate(zip(ps, vs))]
+
     def flat(ref):
         return jnp.concatenate([ref[n] for n in range(samples)], axis=1)
 
     def turned(ks):
-        return jnp.concatenate([k.astype(f32) for k in ks], axis=1).T.astype(bf16)
+        return jnp.concatenate([k.astype(bf16) for k in ks], axis=1).T
 
     loads[0].wait()
     total = [kernels[0, a].astype(f32) for a in range(3)]
@@ -92,6 +104,21 @@
         tail = jnp.concatenate([m[3 * CH:, :CH], m[3 * CH:, CH:]], axis=0)
         return jnp.concatenate([m[:3 * CH], tail], axis=1)
 
+    def first(ps, l):
+        weights[l] = turned([kernels[l, a] for a in range(3)])
+        h = jnp.tanh(flat(states.at[l]).astype(f32))
+        slope = STEP * (1.0 - h * h)
+        acts[l] = h.astype(bf16)
+        slopes[l] = slope
+        return step(ps, [cols(q) for q in ps], l)
+
+    loads[1].wait()
+    loads[2].wait()
+    top = flat(boundary.at[0])
+    ps = [boundary[0, n] for n in range(samples)]
+    for l in reversed(range(LD - EARLY, LD)):
+        ps = first(ps, l)
+
     pl.semaphore_wait(barrier, blocks - 1 + parts - 1)
 
     def mean_copy(peer):
@@ -144,7 +171,7 @@
     def adj_forwards():
         return adj_copy(mate, 2, across), adj_copy(across, 3, mate), adj_copy(3 - mate, 4, mate)
 
-    forwards = [(i, n) for i in range(M) for n in (2, 3)]
+    forwards = [(i, n) for i in range(MO) for n in (2, 3)]
 
     def pass_on(count):
         for i, n in forwards[:count]:
@@ -172,22 +199,21 @@
     def _():
         mean_copy(me - 1).start()
 
-    loads[2].wait()
-    for i in range(M):
-        for copy in far_sends(i):
-            copy.start()
+    for i in range(MI):
+        to_near, to_mate = far_sends(i)
+        to_near.start()
+        if i < MO:
+            to_mate.start()
+        else:
+            @pl.when(outer)
+            def _():
+                to_mate.start()
         far[dp, i] = states[LD - 1 - i]
 
-    loads[1].wait()
-    top = flat(boundary.at[0])
-    p = top
-    for l in reversed(range(LD)):
-        weights[l] = turned([kernels[l, a] for a in range(3)])
-        h = jnp.tanh(flat(states.at[l]).astype(f32))
-        slope = STEP * (1.0 - h * h)
-        acts[l] = h.astype(bf16)
-        slopes[l] = slope
-        p = p + slope * conv(weights[l], cols(p))
+    for l in reversed(range(LD - EARLY)):
+        ps = first(ps, l)
+    p = jnp.concatenate(ps, axis=1)
+    mean_w[me] = mean
     coarse = top + 0.5 * conv(mean, cols(top))
     source = p - jnp.where(me == blocks - 1, 0.0, coarse)
     for part in range(2):
@@ -212,12 +238,24 @@
         def _():
             mean_arrival(j).wait_recv()
             forward(j).start()
+            mean_w[j] = unpacked(means[j])
 
     pass_on(1)
-    for l in range(LD - M):
+    for l in range(LD - MI):
         h = acts[l].astype(f32)
         act_rows[l] = jnp.concatenate(
             [rows_down(h).astype(bf16), h.astype(bf16), rows_up(h).astype(bf16)], axis=0)
+
+    for j in reversed(range(2, blocks - 1)):
+        @pl.when(jnp.logical_and(base + 1 < j, core != j % 2))
+        def _():
+            mean_arrival(j).wait_recv()
+            mean_w[j] = unpacked(means[j])
+
+    @pl.when(jnp.logical_and(jnp.logical_not(last), core == 0))
+    def _():
+        mean_arrival(me + 1).wait_recv()
+        mean_w[me + 1] = unpacked(means[me + 1])
 
     @pl.when(last)
     def _():
@@ -238,16 +276,12 @@
         chain[...] = srcs[blocks - 1].astype(f32)
 
     for j in reversed(range(2, blocks - 1)):
-        pass_on(1)
-
-        @pl.when(jnp.logical_and(base + 1 < j, core != j % 2))
-        def _():
-            mean_arrival(j).wait_recv()
+        pass_on(1 if 0 < blocks - 2 - j < 5 else 0)
 
         @pl.when(base + 1 < j)
         def _():
             e = chain[...]
-            e = e + 0.5 * conv(unpacked(means[j]), cols(e))
+            e = e + 0.5 * conv(mean_w[j], cols(e))
             src_arrival(j).wait_recv()
             chain[...] = e + srcs[j].astype(f32)
 
@@ -256,16 +290,15 @@
         e = chain[...]
         swap_out[...] = e
         swap.start()
-        mean_arrival(me + 1).wait_recv()
         src_arrival(me + 1).wait_recv()
-        adj[:, :width] = e + 0.5 * conv(unpacked(means[me + 1]), cols(e)) + srcs[me + 1].astype(f32)
+        adj[:, :width] = e + 0.5 * conv(mean_w[me + 1], cols(e)) + srcs[me + 1].astype(f32)
         swap.wait_recv()
         adj[:, width:] = swap_in[...]
 
     @pl.when(jnp.logical_and(jnp.logical_not(last), core == 1))
     def _():
         e = chain[...]
-        swap_out[...] = e + 0.5 * conv(unpacked(mean_own[...]), cols(e)) + src_own[1].astype(f32)
+        swap_out[...] = e + 0.5 * conv(mean_w[me], cols(e)) + src_own[1].astype(f32)
         swap.start()
         adj[:, width:] = e
         swap.wait_recv()
@@ -283,7 +316,8 @@
         corrected[0, n] = p[:, n * CELLS:(n + 1) * CELLS]
 
     scale = STEP / (samples * parts)
-    chunks = (LD - M) * PIECES
+    chunks = (LD - MO) * PIECES
+    summed = (MI - MO) * PIECES
 
     def hop(src, dst, send, recv, c, peer):
         part = (c // PIECES, pl.ds(c % PIECES * PIECE, PIECE))
@@ -301,7 +335,7 @@
         return hop(whole, from_inner, c_send, c_recv, c, mate)
 
     def put(c, v):
-        l = LD - M - 1 - c // PIECES
+        l = LD - MO - 1 - c // PIECES
         v = v.astype(f32)
         start = c % PIECES * PIECE
         full = min(max(3 * CH - start, 0), PIECE)
@@ -337,28 +371,32 @@
             e = rep[...]
         h = jnp.tanh(jnp.concatenate([far[s, i, n] for s in pair for n in range(samples)], axis=1).astype(f32))
         v = cols(e)
-        if i < M - 1:
+        if i < MI - 1:
             rep[...] = e + STEP * (1.0 - h * h) * conv(weights[l], v)
         h = h.astype(bf16).astype(f32)
         h = jnp.concatenate([rows_down(h).astype(bf16), h.astype(bf16), rows_up(h).astype(bf16)], axis=0)
         return lax.dot_general(v, h, (((1,), (1,)), ((), ())), preferred_element_type=f32) * scale
 
+    def packed(t):
+        low = jnp.concatenate([t[:3 * CH // 2, 2 * CH:], t[3 * CH // 2:, 2 * CH:]], axis=1)
+        return jnp.concatenate([t[:, :2 * CH], low], axis=0).astype(bf16)
+
+    ps = [p[:, n * CELLS:(n + 1) * CELLS] for n in range(samples)]
     for i in range(LD):
         l = LD - 1 - i
-        v = cols(p)
-        p = p + slopes[l] * conv(weights[l], v)
-        if i >= M:
+        vs = [cols(q) for q in ps]
+        ps = step(ps, vs, l)
+        if i >= MI:
+            v = jnp.concatenate(vs, axis=1)
             t = lax.dot_general(v, act_rows[l], (((1,), (1,)), ((), ())), preferred_element_type=f32) * scale
-            own[i - M, :3 * CH] = t[:, :2 * CH].astype(bf16)
-            own[i - M, 3 * CH:] = jnp.concatenate(
-                [t[:3 * CH // 2, 2 * CH:], t[3 * CH // 2:, 2 * CH:]], axis=1).astype(bf16)
+            own[i - MO] = packed(t)
 
             @pl.when(outer)
             def _():
-                for c in range((i - M) * PIECES, (i - M + 1) * PIECES):
+                for c in range((i - MO) * PIECES, (i - MO + 1) * PIECES):
                     to_inner(c).start()
     for n in range(samples):
-        bottoms[0, n] = p[:, n * CELLS:(n + 1) * CELLS]
+        bottoms[0, n] = ps[n]
 
     adj_copy(mate, 0, mate).wait_recv()
 
@@ -369,50 +407,78 @@
         adj_forwards()[1].start()
 
     pass_on(len(forwards))
-    for i in range(M):
+    for i in range(MO):
         far_arrival(mate, i).wait_recv()
 
-    lag = 2
-    for u in range(2 * M):
-        @pl.when(inner)
-        def _():
-            if u < chunks:
-                pair_sum(u)
-            if lag <= u < chunks + lag:
-                full_sum(u - lag)
-            if u == 1:
+    @pl.when(inner)
+    def _():
+        for i in range(MO, MI):
+            for j in range(1, parts):
+                far_arrival(lax.rem(dp + j, parts), i).wait_recv()
+
+    def sums(u):
+        if summed + u < chunks:
+            pair_sum(summed + u)
+        if u >= LAG and summed + u - LAG < chunks:
+            full_sum(summed + u - LAG)
+
+    def accumulate(half_, i):
+        l = LD - 1 - i
+        t = replicated(near if half_ == 0 else 1 - near, i)
+        gs = [t[:, a * CH:(a + 1) * CH] for a in range(3)]
+        if half_ == 1:
+            gs = [grads[l, a] + gs[a] for a in range(3)]
+        if half_ == 1 and i >= MO:
+            g = i - MO
+            v = packed(jnp.concatenate(gs, axis=1))
+            whole[g] = v
+            for c in range(g * PIECES, (g + 1) * PIECES):
+                to_outer(c).start()
+                start = c % PIECES * PIECE
+                put(c, v[start:start + PIECE])
+        else:
+            for a in range(3):
+                grads[l, a] = gs[a]
+
+    def units(half_):
+        for i in range(MO):
+            accumulate(half_, i)
+        if MI > MO:
+            @pl.when(inner)
+            def _():
+                for i in range(MO, MI):
+                    accumulate(half_, i)
+
+    units(0)
+
+    @pl.when(inner)
+    def _():
+        for u in range(chunks - summed + LAG):
+            sums(u)
+            if u == FWD:
                 adj_copy(3 - mate, 0, mate).wait_recv()
                 adj_forwards()[2].start()
 
-        if u == M:
-            @pl.when(outer)
-            def _():
-                for s in (2 - 2 * near, 3 - 2 * near):
-                    adj_copy(s, 0, mate).wait_recv()
-                    for i in range(M):
-                        far_arrival(s, i).wait_recv()
-
-        l = LD - 1 - u % M
-        t = replicated(near if u < M else 1 - near, u % M)
-        for a in range(3):
-            g = t[:, a * CH:(a + 1) * CH]
-            grads[l, a] = g if u < M else grads[l, a] + g
+    @pl.when(outer)
+    def _():
+        for s in (2 - 2 * near, 3 - 2 * near):
+            adj_copy(s, 0, mate).wait_recv()
+            for i in range(MO):
+                far_arrival(s, i).wait_recv()
+
+    units(1)
 
     @pl.when(inner)
     def _():
-        for u in range(2 * M, chunks + lag):
-            if u < chunks:
-                pair_sum(u)
-            if u >= lag:
-                full_sum(u - lag)
         for c in range(chunks):
-            to_across(c).wait_send()
+            if c >= summed:
+                to_across(c).wait_send()
             to_outer(c).wait_send()
         adj_to_across().wait_send()
         for copy in adj_forwards():
             copy.wait_send()
         for n in (2, 3):
-            for i in range(M):
+            for i in range(MO):
                 far_forward(i, n).wait_send()
 
     @pl.when(outer)
@@ -421,13 +487,19 @@
             to_outer(c).wait_recv()
             part = (c // PIECES, pl.ds(c % PIECES * PIECE, PIECE))
             put(c, from_inner[part])
-        for c in range(chunks):
+        for c in range(summed, chunks):
             to_inner(c).wait_send()
 
     adj_to_mate().wait_send()
-    for i in range(M):
-        for copy in far_sends(i):
-            copy.wait_send()
+    for i in range(MI):
+        to_near, to_mate = far_sends(i)
+        to_near.wait_send()
+        if i < MO:
+            to_mate.wait_send()
+        else:
+            @pl.when(outer)
+            def _():
+                to_mate.wait_send()
 
     for lower in range(0, blocks - 2, 2):
         @pl.when(jnp.logical_and(base > lower, me < blocks - 1))
@@ -470,7 +542,7 @@
 def body(blocks, parts, states, kernels, boundary):
     samples = states.shape[1]
     lanes = samples * CELLS
-    chunks = (LD - M) * PIECES
+    chunks = (LD - MO) * PIECES
     vmem = pl.BlockSpec(memory_space=pltpu.VMEM)
     hbm = pl.BlockSpec(memory_space=pltpu.HBM)
     dma = pltpu.SemaphoreType.DMA
@@ -488,21 +560,22 @@
             pltpu.VMEM((LD, 3, 3 * CH, CH), bf16),
             pltpu.VMEM(boundary.shape, f32),
             dma((3,)),
+            pltpu.VMEM((blocks, 3 * CH, 3 * CH), bf16),
             pltpu.VMEM((LD, 3 * CH, 3 * CH), bf16),
             pltpu.VMEM((LD, CH, lanes), f32),
             pltpu.VMEM((LD, CH, lanes), bf16),
-            pltpu.VMEM((LD - M, 3 * CH, lanes), bf16),
+            pltpu.VMEM((LD - MI, 3 * CH, lanes), bf16),
             pltpu.VMEM((9 * CH // 2, 2 * CH), bf16),
             pltpu.VMEM((blocks, 9 * CH // 2, 2 * CH), bf16),
             pltpu.VMEM((2, CH, lanes // 2), bf16),
             pltpu.VMEM((blocks, CH, lanes // 2), bf16),
             pltpu.VMEM((CH, lanes), f32),
             *[pltpu.VMEM((CH, lanes // 2), f32)] * 3,
-            pltpu.VMEM((parts, M, samples, CH, CELLS), bf16),
+            pltpu.VMEM((parts, MI, samples, CH, CELLS), bf16),
             pltpu.VMEM((parts, CH, lanes), bf16),
             pltpu.VMEM((CH, 2 * lanes), f32),
-            *[pltpu.VMEM((LD - M, PACKED, 2 * CH), bf16)] * 6,
-            dma((4, M)), dma((parts, M)), dma((5,)), dma((parts,)),
+            *[pltpu.VMEM((LD - MO, PACKED, 2 * CH), bf16)] * 6,
+            dma((4, MI)), dma((parts, MI)), dma((5,)), dma((parts,)),
             *[dma((blocks,))] * 5, dma, dma,
             *[dma((chunks,))] * 6,
         ],

time: 37.9 us -> 37.8 us (level)
  no operation moved by 1% of the time
where the time goes in v3:
time: 37.8 us; the launch traced here: 37.7 us
  Pallas kernels  37.1 us (98%)
  between operations  0.64 us (2%)
    pallas_call x1, Pallas kernels, body(): pl.pallas_call(functools.partial(kernel, blocks, parts, samples), out_sha...  35.6 us
    pallas_call x1, Pallas kernels, body(): pl.pallas_call(write, out_shape=tuple((jax.ShapeDtypeStruct(a.shape, a.dt...  1.5 us

profile of v3, /device:TPU:0, one launch (start us, length us, event | category | flops | bytes accessed | tf_op | source)
XLA Modules:
  0.0 37.7 jit_solution(6714156480245461163)
XLA Ops:
  0.6 35.6 %cycle.1 = (f32[1,2,64,256]{3,2,1,0:T(8,128)S(1)}, f32[1,2,64,256]{3,2,1,0:T(8,128)S(1)}, f32[8,3,192,64]{3,2,1,0:T(8,128)S(1)}) custom-call(bf16[8,2,64,256]{3,2,1,0:T(8,128)(2,1)} %states_in.1, bf16[8,3,192,64]{3,2,1,0:T(8,128)(2,1)} %bitcast.3, f32[1,2,64,256]{3,2,1,0:T(8,128)} %boundary_in.1), custom_call_target="tpu_custom_call" | custom-call | flops 2000000000 | bytes 6000000 | tf_op jit(solution)/shard_map/cycle/pallas_call | solution.py:549
  36.2 1.5 %write.1 = (f32[1,2,64,256]{3,2,1,0:T(8,128)}, f32[1,2,64,256]{3,2,1,0:T(8,128)}, f32[8,3,192,64]{3,2,1,0:T(8,128)}) custom-call(f32[1,2,64,256]{3,2,1,0:T(8,128)S(1)} %get-tuple-element.9.corrected, f32[1,2,64,256]{3,2,1,0:T(8,128)S(1)} %get-tuple-element.10.bottoms, f32[8,3,192,64]{3,2,1,0:T(8,128)S(1)} %get-tuple-element.11.grads), custom_call_target="tpu_custom_call" | custom-call | bytes 5000000 | tf_op jit(solution)/shard_map/write/pallas_call | solution.py:588

commit v4 on v3

--- a/solution.py
+++ b/solution.py
@@ -201,13 +201,8 @@
 
     for i in range(MI):
         to_near, to_mate = far_sends(i)
+        to_mate.start()
         to_near.start()
-        if i < MO:
-            to_mate.start()
-        else:
-            @pl.when(outer)
-            def _():
-                to_mate.start()
         far[dp, i] = states[LD - 1 - i]
 
     for l in reversed(range(LD - EARLY)):

time: 37.8 us -> 37 us (0.979)
  Pallas kernels: 37.1 us -> 36.2 us
    pallas_call x1, Pallas kernels: 35.6 us -> 34.7 us  [body(): pl.pallas_call(functools.partial(kernel, blocks, parts, samples), out_sha...]
where the time goes in v4:
time: 37 us; the launch traced here: 36.8 us
  Pallas kernels  36.2 us (98%)
  between operations  0.64 us (2%)
    pallas_call x1, Pallas kernels, body(): pl.pallas_call(functools.partial(kernel, blocks, parts, samples), out_sha...  34.7 us
    pallas_call x1, Pallas kernels, body(): pl.pallas_call(write, out_shape=tuple((jax.ShapeDtypeStruct(a.shape, a.dt...  1.5 us

profile of v4, /device:TPU:0, one launch (start us, length us, event | category | flops | bytes accessed | tf_op | source)
XLA Modules:
  0.0 36.8 jit_solution(3921135978545365419)
XLA Ops:
  0.6 34.7 %cycle.1 = (f32[1,2,64,256]{3,2,1,0:T(8,128)S(1)}, f32[1,2,64,256]{3,2,1,0:T(8,128)S(1)}, f32[8,3,192,64]{3,2,1,0:T(8,128)S(1)}) custom-call(bf16[8,2,64,256]{3,2,1,0:T(8,128)(2,1)} %states_in.1, bf16[8,3,192,64]{3,2,1,0:T(8,128)(2,1)} %bitcast.3, f32[1,2,64,256]{3,2,1,0:T(8,128)} %boundary_in.1), custom_call_target="tpu_custom_call" | custom-call | flops 2000000000 | bytes 6000000 | tf_op jit(solution)/shard_map/cycle/pallas_call | solution.py:544
  35.3 1.5 %write.1 = (f32[1,2,64,256]{3,2,1,0:T(8,128)}, f32[1,2,64,256]{3,2,1,0:T(8,128)}, f32[8,3,192,64]{3,2,1,0:T(8,128)}) custom-call(f32[1,2,64,256]{3,2,1,0:T(8,128)S(1)} %get-tuple-element.9.corrected, f32[1,2,64,256]{3,2,1,0:T(8,128)S(1)} %get-tuple-element.10.bottoms, f32[8,3,192,64]{3,2,1,0:T(8,128)S(1)} %get-tuple-element.11.grads), custom_call_target="tpu_custom_call" | custom-call | bytes 5000000 | tf_op jit(solution)/shard_map/write/pallas_call | solution.py:583
